TPU v7x, 256 devices: a whole 4x4x8 slice. The times are simulated.
256 devices in a mesh: row: 8 (over z), col: 4 (over y_lo, core), depth: 8 (over y_hi, x).
Axes of the slice: x: 4, y: 4 (y_hi: 2, y_lo: 2; y = y_hi * 2 + y_lo), z: 8, core: 2. Of those that a mesh axis runs over, the one named last changes fastest.
Arguments:
- tokens: bfloat16 [1536, 12288], P(('row', 'col'), 'depth'), may hold values from -6 to 6
- up_weight: bfloat16 [12288, 24576], P('depth', ('row', 'col')), may hold values from -0.0546875 to 0.0546875
- up_bias: float32 [24576], P(('row', 'col')), may hold values from -3 to 3
- down_weight: bfloat16 [24576, 12288], P(('row', 'col'), 'depth'), may hold values from -0.0390625 to 0.0390625
- down_bias: float32 [12288], P('depth'), may hold values from -3 to 3
Outputs:
- layer_out: bfloat16 [1536, 12288], P(('row', 'col'), 'depth')
All inputs are finite; a program needn't handle non-finite values.
Results may differ from a plain program's by a relative error of at most 0.0043.
Values may be sent and summed in bfloat16 or wider, within the bound.
A program may use at most 64 MiB of HBM per device.

v0:
```python
import jax
import jax.numpy as jnp
from jax import lax
from jax.sharding import PartitionSpec as P


def per_device(tokens, up_weight, up_bias, down_weight, down_bias):
    partial_pre = jnp.dot(
        lax.all_gather(tokens, ("row", "col"), axis=0, tiled=True),
        up_weight,
        preferred_element_type=jnp.float32,
    )
    pre_act = lax.psum(partial_pre, "depth") + up_bias
    activated = jax.nn.gelu(pre_act, approximate=True).astype(jnp.bfloat16)
    summed = lax.psum_scatter(
        jnp.dot(activated, down_weight, preferred_element_type=jnp.float32),
        ("row", "col"),
        scatter_dimension=0,
        tiled=True,
    )
    return (summed + down_bias).astype(jnp.bfloat16)


def solution(mesh):
    return jax.shard_map(
        per_device,
        mesh=mesh,
        in_specs=(
            P(("row", "col"), "depth"),
            P("depth", ("row", "col")),
            P(("row", "col")),
            P(("row", "col"), "depth"),
            P("depth"),
        ),
        out_specs=P(("row", "col"), "depth"),
        check_vma=False,
    )
```

profile of v0, /device:TPU:8, one launch (start us, length us, event | category | flops | bytes accessed | tf_op | source)
XLA Modules:
  0.0 357.1 jit_solution(10681562351338968876)
XLA Ops:
  6.5 0.0 copy-start
  6.5 0.0 all-gather.2.cloned.1.call-start
  6.5 0.7 all-gather.2.cloned.1.call-update
  7.3 0.0 all-reduce.2.cloned.1.call-start
  7.3 72.3 %all-gather.2.cloned.1.call-done = bf16[1536,1536]{1,0:T(8,128)(2,1)} async-done(((bf16[48,1536]{1,0:T(8,128)(2,1)}), bf16[1536,1536]{1,0:T(8,128)(2,1)}) %all-gather.2.cloned.1.call-update) | async-done | bytes 4718608 | tf_op jit(solution)/shard_map/all_gather | solution.py:9
  79.6 9.1 %fusion.19 = f32[1536,768]{1,0:T(8,128)} fusion(bf16[1536,1536]{1,0:T(8,128)(2,1)} %all-gather.2.cloned.1.call-done, bf16[1536,768]{1,0:T(8,128)(2,1)} %param.6), kind=kOutput, calls=%fused_computation.20 | convolution fusion | flops 3623878656 | bytes 11796480 | tf_op jit(solution)/shard_map/dot_general | solution.py:8
  88.7 0.0 copy-start.2
  88.7 0.0 all-reduce.2.cloned.1.call-update
  88.7 0.0 reduce-scatter.2.cloned.1.call-start
  88.7 121.7 %all-reduce.2.cloned.1.call-done = f32[1536,768]{1,0:T(8,128)} async-done(((f32[1536,768]{1,0:T(8,128)}), f32[1536,768]{1,0:T(8,128)}) %all-reduce.2.cloned.1.call-update) | async-done | bytes 4718608 | tf_op jit(solution)/shard_map/psum | solution.py:13
  210.5 0.0 copy-done
  210.5 0.0 copy-done.2
  210.5 10.7 %fusion.8 = f32[1536,1536]{1,0:T(8,128)} fusion(bf16[768,1536]{1,0:T(8,128)(2,1)S(1)} %copy-done, f32[1536,768]{1,0:T(8,128)} %all-reduce.2.cloned.1.call-done, f32[768]{0:T(1024)S(1)} %copy-done.2), kind=kOutput, calls=%fused_computation.9 | convolution fusion | flops 3635675136 | bytes 16518144 | tf_op jit(solution)/shard_map/dot_general | solution.py:16
  221.2 0.0 copy-start.1
  221.2 0.0 reduce-scatter.2.cloned.1.call-update
  221.2 127.7 %reduce-scatter.2.cloned.1.call-done = f32[48,1536]{1,0:T(8,128)} async-done(((f32[1536,1536]{1,0:T(8,128)}), f32[48,1536]{1,0:T(8,128)}) %reduce-scatter.2.cloned.1.call-update) | async-done | bytes 294928 | tf_op jit(solution)/shard_map/reduce_scatter | solution.py:15
  348.9 0.0 copy-done.1
  348.9 1.6 add_convert_fusion
Async XLA Ops:
  6.5 204.0 %copy-start = (bf16[768,1536]{1,0:T(8,128)(2,1)S(1)}, bf16[768,1536]{1,0:T(8,128)(2,1)}, u32[]{:S(2)}) copy-start(bf16[768,1536]{1,0:T(8,128)(2,1)} %param.8) | copy-start | bytes 7077892
  6.5 73.1 %all-gather.2.cloned.1.call-start = ((), (), s32[]{:S(2)}) async-start(), calls=%async_computation.1 | async-start | bytes 4866048 | tf_op jit(solution)/shard_map/all_gather | solution.py:9
  7.3 203.2 %all-reduce.2.cloned.1.call-start = ((), (), s32[]{:S(2)}) async-start(), calls=%async_computation.2 | async-start | bytes 9437184 | tf_op jit(solution)/shard_map/psum | solution.py:13
  88.7 121.8 %copy-start.2 = (f32[768]{0:T(1024)S(1)}, f32[768]{0:T(1024)}, u32[]{:S(2)}) copy-start(f32[768]{0:T(1024)} %param.7) | copy-start | bytes 9220
  88.7 260.2 %reduce-scatter.2.cloned.1.call-start = ((), (), s32[]{:S(2)}) async-start(), calls=%async_computation.3 | async-start | bytes 9732096 | tf_op jit(solution)/shard_map/reduce_scatter | solution.py:15
  221.2 127.7 %copy-start.1 = (f32[1536]{0:T(1024)S(1)}, f32[1536]{0:T(1024)}, u32[]{:S(2)}) copy-start(f32[1536]{0:T(1024)} %param.9) | copy-start | bytes 18436
Sparse Core Ops, SparseCore 0:
  9.2 70.3 all-gather.1
  88.8 121.6 all-reduce.1
  221.4 127.4 reduce-scatter.1
where the time goes:
time: 361 us; the launch traced here: 357 us
  waiting for transfers between devices  322 us (89%)
  matrix products  19.8 us (5%)
  between operations  13.1 us (4%)
    reduce_scatter x1, waiting for transfers between devices, per_device(): lax.psum_scatter(jnp.dot(activated, down_weight, preferred_element_type=j...  128 us
    psum x1, waiting for transfers between devices, per_device(): pre_act = lax.psum(partial_pre, 'depth') + up_bias  122 us
    all_gather x1, waiting for transfers between devices, per_device(): lax.all_gather(tokens, ('row', 'col'), axis=0, tiled=True)  72.3 us
    dot_general x1, matrix products, per_device(): jnp.dot(activated, down_weight, preferred_element_type=jnp.float32)  10.7 us
    dot_general x1, matrix products, per_device(): jnp.dot(lax.all_gather(tokens, ('row', 'col'), axis=0, tiled=True), up_we...  9.07 us
  transfers between devices with their start and end apart: 3, of which 3 were waited for; matrix products, arithmetic and copies ran while one was open for 0% of the time, Pallas kernels for 0%

commit v1 on v0

v1 whole, which is shorter than its diff:
```python
import jax
import jax.numpy as jnp
from jax import lax
from jax.experimental import pallas as pl
from jax.experimental.pallas import tpu as pltpu
from jax.sharding import PartitionSpec as P

NC = 3
RB = 16
NZ = 8
ORDER = (
    (0, 1, 0), (0, 2, 0), (0, 0, 0), (0, 1, 1), (0, 2, 1), (1, 2, 0), (1, 1, 0), (0, 1, 2), (0, 2, 2),
    (1, 1, 1), (0, 1, 3), (1, 2, 1), (2, 2, 0), (0, 2, 3), (1, 1, 2), (2, 1, 0), (0, 0, 1), (1, 2, 2),
    (3, 2, 0), (0, 1, 4), (0, 2, 4), (1, 0, 0), (1, 1, 3), (2, 1, 2), (0, 1, 5), (0, 0, 2), (1, 2, 3),
    (2, 2, 2), (0, 2, 5), (1, 2, 4), (0, 0, 3), (2, 1, 3), (1, 1, 4), (1, 0, 1), (2, 2, 4), (0, 0, 4),
    (3, 1, 2), (2, 1, 4), (2, 2, 3), (4, 2, 0), (1, 0, 3), (2, 1, 1), (0, 0, 5), (3, 2, 4), (3, 1, 4),
    (1, 0, 4), (1, 0, 2), (2, 0, 3), (3, 2, 3), (3, 1, 3), (4, 2, 4), (4, 1, 4), (2, 0, 4), (2, 2, 1),
    (5, 2, 4), (4, 1, 2), (2, 0, 2), (5, 1, 4), (3, 0, 4), (3, 2, 2), (3, 0, 3), (2, 0, 0), (4, 2, 3),
    (2, 0, 1), (3, 2, 1), (4, 1, 3), (5, 2, 3), (3, 0, 2), (4, 0, 4), (5, 1, 3), (4, 2, 2), (3, 1, 0),
    (5, 0, 4), (4, 0, 3), (5, 2, 2), (3, 0, 1), (4, 2, 1), (5, 0, 3), (4, 0, 2), (5, 2, 1), (3, 1, 1),
    (4, 1, 0), (5, 0, 2), (4, 0, 1), (3, 0, 0), (5, 1, 2), (4, 1, 1), (5, 0, 1), (4, 0, 0), (5, 2, 0),
    (5, 1, 1), (5, 0, 0), (5, 1, 0), (6, 0, 0), (6, 2, 0), (6, 1, 0),
)
CORE = jnp.float32
MESH = pl.DeviceIdType.MESH
GROUPS = ((0, 1), (1, 2), (3, 2), (5, 2), (7, 1))


def kernel(
    tok, w1_hbm, b1, w2_hbm, b2, out,
    G, W1, W2, XF, XS, XR, YS, YR, A, OF, CS, CR, ZS, ZR, FS, LS, LR,
    load_sem, ss, rs,
):
    z = lax.axis_index("row")
    col = lax.axis_index("col")
    dep = lax.axis_index("depth")
    yl, c = col // 2, col % 2
    yh, x = dep // 4, dep % 4

    up_z = ((z + 1) % NZ, col, dep)
    dn_z = ((z + NZ - 1) % NZ, col, dep)
    mate = (z, yl * 2 + (1 - c), dep)
    near_y = (z, (1 - yl) * 2 + c, dep)
    far_y = (z, col, (1 - yh) * 4 + x)
    xs = [(x + d) % 4 for d in (1, 2, 3)]
    x_dev = [(z, col, yh * 4 + xd) for xd in xs]

    loads = [
        pltpu.make_async_copy(tok.at[pl.ds(k * RB, RB)], G.at[k, 0, c, yl], load_sem.at[k])
        for k in range(NC)
    ]
    loads.append(pltpu.make_async_copy(w1_hbm, W1, load_sem.at[NC]))
    loads.append(pltpu.make_async_copy(w2_hbm, W2, load_sem.at[NC + 1]))
    for copy in loads:
        copy.start()

    barrier = pltpu.get_barrier_semaphore()
    peers = [up_z, dn_z, mate, near_y, far_y] + x_dev
    for dev in peers:
        pl.semaphore_signal(barrier, inc=1, device_id=dev, device_id_type=MESH)
    pl.semaphore_wait(barrier, len(peers))

    copies = {}
    waited = set()

    def send(name, src, dst, dev):
        i = len(copies)
        copy = pltpu.make_async_remote_copy(
            src_ref=src, dst_ref=dst, send_sem=ss.at[i], recv_sem=rs.at[i],
            device_id=dev, device_id_type=MESH,
        )
        copy.start()
        copies[name] = copy

    def arrived(*name):
        copies[name].wait_recv()

    def to_mate(k, g):
        s, n = GROUPS[g]
        part = G.at[k, pl.ds(s, n), c]
        send(("mate", k, g), part, part, mate)

    def gather(k, step):
        if step == 0:
            loads[k].wait()
            own = G.at[k, 0, c, yl]
            send(("near", k), own, own, near_y)
        elif step == 1:
            arrived("near", k)
            send(("up", k, 1), G.at[k, 0, c], G.at[k, 1, c], up_z)
            send(("dn", k, 1), G.at[k, 0, c], G.at[k, 2, c], dn_z)
            to_mate(k, 0)
        elif step < 4:
            arrived("up", k, step - 1)
            s = 2 * step - 3
            send(("up", k, step), G.at[k, s, c], G.at[k, s + 2, c], up_z)
            arrived("dn", k, step - 1)
            send(("dn", k, step), G.at[k, s + 1, c], G.at[k, s + 3, c], dn_z)
            to_mate(k, step - 1)
        elif step == 4:
            arrived("up", k, 3)
            send(("up", k, 4), G.at[k, 5, c, 0], G.at[k, 7, c, 0], up_z)
            arrived("dn", k, 3)
            send(("dn", k, 4), G.at[k, 6, c, 1], G.at[k, 7, c, 1], dn_z)
            to_mate(k, 3)
        else:
            arrived("up", k, 4)
            arrived("dn", k, 4)
            to_mate(k, 4)

    def up_proj(k, g):
        s, n = GROUPS[g]
        if NC not in waited:
            waited.add(NC)
            loads[NC].wait()
        arrived("mate", k, g)

        @pl.loop(0, 3)
        def _(t):
            cols = pl.ds(pl.multiple_of(t * 256, 256), 256)
            lhs = G[k, pl.ds(s, n)].reshape(n * 4 * RB, 1536)
            r = jnp.dot(lhs, W1[:, cols], preferred_element_type=jnp.float32)
            r = r.reshape(n, 4, RB, 256)
            for i in range(n):
                for j in range(4):
                    XF[k, j, s + i, :, cols] = r[i, j]
                    XS[k, j, s + i, :, cols] = r[i, j].astype(jnp.bfloat16)

        for d in (1, 0, 2):
            send(("xs", k, g, d), XS.at[k, xs[d], pl.ds(s, n)], XR.at[k, d, pl.ds(s, n)], x_dev[d])

    def x_sum(k, g):
        s, n = GROUPS[g]
        for d in range(3):
            arrived("xs", k, g, d)
        rows = pl.ds(s, n)
        total = XF[k, x, rows]
        for d in range(3):
            total = total + XR[k, d, rows].astype(jnp.float32)
        YS[k, rows] = total
        send(("far", k, g), YS.at[k, rows], YR.at[k, rows], far_y)

    def activate(k, g):
        s, n = GROUPS[g]
        arrived("far", k, g)
        rows = pl.ds(s, n)
        v = YS[k, rows] + YR[k, rows] + b1[...].reshape(1, 1, 768)
        A[k, x, rows] = jax.nn.gelu(v, approximate=True).astype(jnp.bfloat16)
        for d in (1, 0, 2):
            send(("act", k, g, d), A.at[k, x, rows], A.at[k, x, rows], x_dev[d])

    def down_proj(k, g):
        s, n = GROUPS[g]
        if NC + 1 not in waited:
            waited.add(NC + 1)
            loads[NC + 1].wait()
        for d in range(3):
            arrived("act", k, g, d)
        first = c == 0

        @pl.loop(0, 6)
        def _(t):
            cols = pl.ds(pl.multiple_of(t * 256, 256), 256)
            lhs = A[k, :, pl.ds(s, n)].reshape(4 * n * RB, 768)
            r = jnp.dot(lhs, W2[:, cols], preferred_element_type=jnp.float32)
            r = r.reshape(2, 2, n, RB, 256)
            mine = jnp.where(first, r[0], r[1])
            other = jnp.where(first, r[1], r[0]).astype(CORE)
            for i in range(n):
                for j in range(2):
                    OF[k, s + i, j, :, cols] = mine[j, i]
                    CS[k, s + i, j, :, cols] = other[j, i]

        send(("core", k, g), CS.at[k, pl.ds(s, n)], CR.at[k, pl.ds(s, n)], mate)

    def reduce_z(k, g):
        s, n = GROUPS[g]
        arrived("core", k, g)

        def term(slot, block):
            return OF[k, slot, block] + CR[k, slot, block].astype(jnp.float32)

        if g == 4:
            for b in range(2):
                ZS[k, 7, b] = term(7, b).astype(jnp.bfloat16)
            send(("zdn", k, 4), ZS.at[k, 7, 0], ZR.at[k, 5, 0], dn_z)
            send(("zup", k, 4), ZS.at[k, 7, 1], ZR.at[k, 6, 1], up_z)
        elif g > 0:
            for name, slot, dev, there in (("zdn", s, dn_z, (s - 2) if g > 1 else 0), ("zup", s + 1, up_z, (s - 1) if g > 1 else 7)):
                arrived(name, k, g + 1)
                for b in range(2):
                    v = term(slot, b)
                    if g < 3 or b == (0 if name == "zdn" else 1):
                        v = v + ZR[k, slot, b].astype(jnp.float32)
                    ZS[k, slot, b] = v.astype(jnp.bfloat16)
                send((name, k, g), ZS.at[k, slot], ZR.at[k, there], dev)
        else:
            arrived("zdn", k, 1)
            arrived("zup", k, 1)
            for b in range(2):
                FS[k, b] = term(0, b) + ZR[k, 0, b].astype(jnp.float32) + ZR[k, 7, b].astype(jnp.float32)
            LS[k] = FS[k, 1 - yl]
            send(("last", k), LS.at[k], LR.at[k], near_y)

    def finish(k):
        arrived("last", k)
        v = FS[k, yl] + LR[k] + b2[...]
        out[pl.ds(k * RB, RB)] = v.astype(jnp.bfloat16)

    what = (gather, up_proj, x_sum, activate, down_proj, reduce_z, finish)
    for w, k, i in ORDER:
        what[w](*((k,) if w == 6 else (k, i)))

    for copy in copies.values():
        copy.wait_send()


def per_device(tokens, up_weight, up_bias, down_weight, down_bias):
    f32, bf16 = jnp.float32, jnp.bfloat16
    any_spec = pl.BlockSpec(memory_space=pl.ANY)
    vmem = pl.BlockSpec(memory_space=pltpu.VMEM)
    n_copies = NC * 64
    return pl.pallas_call(
        kernel,
        out_shape=jax.ShapeDtypeStruct((48, 1536), bf16),
        in_specs=[any_spec, any_spec, vmem, any_spec, vmem],
        out_specs=vmem,
        scratch_shapes=[
            pltpu.VMEM((NC, NZ, 2, 2, RB, 1536), bf16),
            pltpu.VMEM((1536, 768), bf16),
            pltpu.VMEM((768, 1536), bf16),
            pltpu.VMEM((NC, 4, NZ, RB, 768), f32),
            pltpu.VMEM((NC, 4, NZ, RB, 768), bf16),
            pltpu.VMEM((NC, 3, NZ, RB, 768), bf16),
            pltpu.VMEM((NC, NZ, RB, 768), f32),
            pltpu.VMEM((NC, NZ, RB, 768), f32),
            pltpu.VMEM((NC, 4, NZ, RB, 768), bf16),
            pltpu.VMEM((NC, NZ, 2, RB, 1536), f32),
            pltpu.VMEM((NC, NZ, 2, RB, 1536), CORE),
            pltpu.VMEM((NC, NZ, 2, RB, 1536), CORE),
            pltpu.VMEM((NC, NZ, 2, RB, 1536), bf16),
            pltpu.VMEM((NC, NZ, 2, RB, 1536), bf16),
            pltpu.VMEM((NC, 2, RB, 1536), f32),
            pltpu.VMEM((NC, RB, 1536), f32),
            pltpu.VMEM((NC, RB, 1536), f32),
            pltpu.SemaphoreType.DMA((NC + 2,)),
            pltpu.SemaphoreType.DMA((n_copies,)),
            pltpu.SemaphoreType.DMA((n_copies,)),
        ],
        compiler_params=pltpu.CompilerParams(
            collective_id=0, has_side_effects=True, vmem_limit_bytes=56 * 2**20
        ),
        cost_estimate=pl.CostEstimate(flops=7_300_000_000, bytes_accessed=5_000_000, transcendentals=600_000),
    )(tokens, up_weight, up_bias.reshape(1, 768), down_weight, down_bias.reshape(1, 1536))


def solution(mesh):
    return jax.shard_map(
        per_device,
        mesh=mesh,
        in_specs=(
            P(("row", "col"), "depth"),
            P("depth", ("row", "col")),
            P(("row", "col")),
            P(("row", "col"), "depth"),
            P("depth"),
        ),
        out_specs=P(("row", "col"), "depth"),
        check_vma=False,
    )
```

time: 361 us -> 95 us (0.26); the launches traced: 357 us -> 94.8 us
  waiting for transfers between devices: 322 us -> 0 us
  Pallas kernels: 0 us -> 90.6 us
  matrix products: 19.8 us -> 0 us
  between operations: 13.1 us -> 0.01 us
  local copies, waits for them, and re-layouts: 0.01 us -> 4.16 us
    reduce_scatter x1 -> x0, waiting for transfers between devices: 128 us -> none  [per_device(): lax.psum_scatter(jnp.dot(activated, down_weight, preferred_element_type=j...]
    psum x1 -> x0, waiting for transfers between devices: 122 us -> none  [per_device(): pre_act = lax.psum(partial_pre, 'depth') + up_bias]
    pallas_call x0 -> x1, Pallas kernels: none -> 90.6 us  [per_device(): pl.pallas_call(kernel, out_shape=jax.ShapeDtypeStruct((48, 1536), bf16),...]
    all_gather x1 -> x0, waiting for transfers between devices: 72.3 us -> none  [per_device(): lax.all_gather(tokens, ('row', 'col'), axis=0, tiled=True)]
    dot_general x2 -> x0, matrix products: 19.8 us -> none  [the longest x1 10.7 us: per_device(): jnp.dot(activated, down_weight, preferred_element_type=jnp.float32)]
  transfers between devices with their start and end apart: 3 -> 0, of which waited for: 3 -> 0; matrix products, arithmetic and copies ran while one was open for 0% -> 0% of each run, Pallas kernels for 0% -> 0%
where the time goes in v1:
time: 95 us; the launch traced here: 94.8 us
  Pallas kernels  90.6 us (95%)
  local copies, waits for them, and re-layouts  4.16 us (4%)
    pallas_call x1, Pallas kernels, per_device(): pl.pallas_call(kernel, out_shape=jax.ShapeDtypeStruct((48, 1536), bf16),...  90.6 us

profile of v1, /device:TPU:8, one launch (start us, length us, event | category | flops | bytes accessed | tf_op | source)
XLA Modules:
  0.0 94.8 jit_solution(5677667834206416815)
XLA Ops:
  0.0 1.3 %reshape.6.b1 = f32[1,768]{1,0:T(1,128)} reshape(f32[768]{0:T(1024)} %param.7) | data formatting | bytes 6144 | tf_op jit(solution)/shard_map/reshape | solution.py:254
  1.3 1.3 %reshape.7.b2 = f32[1,1536]{1,0:T(1,128)} reshape(f32[1536]{0:T(1024)} %param.9) | data formatting | bytes 12288 | tf_op jit(solution)/shard_map/reshape | solution.py:254
  2.6 90.6 %shard_map.55 = bf16[48,1536]{1,0:T(8,128)(2,1)} custom-call(bf16[48,1536]{1,0:T(8,128)(2,1)} %tok.1, bf16[1536,768]{1,0:T(8,128)(2,1)} %w1_hbm.1, f32[1,768]{1,0:T(1,128)} %reshape.6.b1, bf16[768,1536]{1,0:T(8,128)(2,1)} %w2_hbm.1, f32[1,1536]{1,0:T(1,128)} %reshape.7.b2), custom_call_target="tpu_custom_call" | custom-call | flops 7299999744 | bytes 5000000 | tf_op jit(solution)/shard_map/pallas_call | solution.py:223
  93.2 1.6 %copy.7 = bf16[48,1536]{1,0:T(8,128)(2,1)} copy(bf16[48,1536]{1,0:T(8,128)(2,1)} %shard_map.55) | data formatting | bytes 294912

commit v2 on v1

--- a/solution.py
+++ b/solution.py
@@ -9,17 +9,17 @@
 RB = 16
 NZ = 8
 ORDER = (
-    (0, 1, 0), (0, 2, 0), (0, 0, 0), (0, 1, 1), (0, 2, 1), (1, 2, 0), (1, 1, 0), (0, 1, 2), (0, 2, 2),
-    (1, 1, 1), (0, 1, 3), (1, 2, 1), (2, 2, 0), (0, 2, 3), (1, 1, 2), (2, 1, 0), (0, 0, 1), (1, 2, 2),
-    (3, 2, 0), (0, 1, 4), (0, 2, 4), (1, 0, 0), (1, 1, 3), (2, 1, 2), (0, 1, 5), (0, 0, 2), (1, 2, 3),
-    (2, 2, 2), (0, 2, 5), (1, 2, 4), (0, 0, 3), (2, 1, 3), (1, 1, 4), (1, 0, 1), (2, 2, 4), (0, 0, 4),
-    (3, 1, 2), (2, 1, 4), (2, 2, 3), (4, 2, 0), (1, 0, 3), (2, 1, 1), (0, 0, 5), (3, 2, 4), (3, 1, 4),
-    (1, 0, 4), (1, 0, 2), (2, 0, 3), (3, 2, 3), (3, 1, 3), (4, 2, 4), (4, 1, 4), (2, 0, 4), (2, 2, 1),
-    (5, 2, 4), (4, 1, 2), (2, 0, 2), (5, 1, 4), (3, 0, 4), (3, 2, 2), (3, 0, 3), (2, 0, 0), (4, 2, 3),
-    (2, 0, 1), (3, 2, 1), (4, 1, 3), (5, 2, 3), (3, 0, 2), (4, 0, 4), (5, 1, 3), (4, 2, 2), (3, 1, 0),
-    (5, 0, 4), (4, 0, 3), (5, 2, 2), (3, 0, 1), (4, 2, 1), (5, 0, 3), (4, 0, 2), (5, 2, 1), (3, 1, 1),
-    (4, 1, 0), (5, 0, 2), (4, 0, 1), (3, 0, 0), (5, 1, 2), (4, 1, 1), (5, 0, 1), (4, 0, 0), (5, 2, 0),
-    (5, 1, 1), (5, 0, 0), (5, 1, 0), (6, 0, 0), (6, 2, 0), (6, 1, 0),
+    (0, 0, 0), (0, 2, 0), (0, 1, 0), (0, 0, 1), (1, 0, 0), (0, 2, 1), (0, 0, 2), (1, 2, 0), (0, 2, 2),
+    (1, 0, 1), (0, 1, 1), (1, 2, 1), (0, 0, 3), (1, 1, 0), (1, 0, 2), (2, 0, 0), (0, 2, 3), (1, 2, 2),
+    (0, 1, 2), (2, 0, 1), (0, 0, 4), (3, 0, 0), (2, 1, 0), (2, 2, 1), (0, 2, 4), (1, 0, 3), (0, 1, 3),
+    (1, 1, 1), (0, 0, 5), (0, 2, 5), (2, 2, 2), (1, 0, 4), (2, 2, 0), (1, 2, 4), (0, 1, 4), (1, 2, 3),
+    (2, 0, 3), (1, 1, 3), (0, 1, 5), (2, 2, 4), (2, 0, 4), (1, 1, 4), (2, 2, 3), (3, 0, 3), (3, 2, 4),
+    (4, 0, 0), (3, 0, 4), (2, 1, 4), (2, 1, 3), (1, 1, 2), (2, 0, 2), (4, 0, 3), (3, 1, 4), (3, 2, 3),
+    (4, 0, 4), (4, 2, 4), (3, 1, 3), (5, 0, 4), (2, 1, 2), (2, 1, 1), (4, 1, 4), (3, 0, 2), (5, 2, 4),
+    (3, 2, 2), (5, 1, 4), (4, 2, 3), (5, 0, 3), (3, 1, 2), (4, 1, 3), (5, 2, 3), (3, 0, 1), (4, 0, 2),
+    (3, 2, 1), (5, 1, 3), (4, 2, 2), (5, 0, 2), (3, 1, 1), (4, 1, 2), (5, 2, 2), (4, 0, 1), (5, 1, 2),
+    (3, 2, 0), (4, 2, 1), (5, 0, 1), (4, 1, 1), (5, 2, 1), (3, 1, 0), (4, 2, 0), (5, 1, 1), (5, 0, 0),
+    (4, 1, 0), (5, 2, 0), (5, 1, 0), (6, 0, 0), (6, 2, 0), (6, 1, 0),
 )
 CORE = jnp.float32
 MESH = pl.DeviceIdType.MESH

time: 95 us -> 92.5 us (0.974)
  Pallas kernels: 90.6 us -> 87.5 us
    pallas_call x1, Pallas kernels: 90.6 us -> 87.5 us  [per_device(): pl.pallas_call(kernel, out_shape=jax.ShapeDtypeStruct((48, 1536), bf16),...]
where the time goes in v2:
time: 92.5 us; the launch traced here: 91.7 us
  Pallas kernels  87.5 us (95%)
  local copies, waits for them, and re-layouts  4.16 us (4%)
    pallas_call x1, Pallas kernels, per_device(): pl.pallas_call(kernel, out_shape=jax.ShapeDtypeStruct((48, 1536), bf16),...  87.5 us

profile of v2, /device:TPU:8, one launch (start us, length us, event | category | flops | bytes accessed | tf_op | source)
XLA Modules:
  0.0 91.7 jit_solution(8355998853801035377)
XLA Ops:
  0.0 1.3 %reshape.6.b1 = f32[1,768]{1,0:T(1,128)} reshape(f32[768]{0:T(1024)} %param.7) | data formatting | bytes 6144 | tf_op jit(solution)/shard_map/reshape | solution.py:254
  1.3 1.3 %reshape.7.b2 = f32[1,1536]{1,0:T(1,128)} reshape(f32[1536]{0:T(1024)} %param.9) | data formatting | bytes 12288 | tf_op jit(solution)/shard_map/reshape | solution.py:254
  2.6 87.5 %shard_map.55 = bf16[48,1536]{1,0:T(8,128)(2,1)} custom-call(bf16[48,1536]{1,0:T(8,128)(2,1)} %tok.1, bf16[1536,768]{1,0:T(8,128)(2,1)} %w1_hbm.1, f32[1,768]{1,0:T(1,128)} %reshape.6.b1, bf16[768,1536]{1,0:T(8,128)(2,1)} %w2_hbm.1, f32[1,1536]{1,0:T(1,128)} %reshape.7.b2), custom_call_target="tpu_custom_call" | custom-call | flops 7299999744 | bytes 5000000 | tf_op jit(solution)/shard_map/pallas_call | solution.py:223
  90.1 1.6 %copy.7 = bf16[48,1536]{1,0:T(8,128)(2,1)} copy(bf16[48,1536]{1,0:T(8,128)(2,1)} %shard_map.55) | data formatting | bytes 294912
